TPU v7x, 128 devices: a whole 4x4x4 slice. The times are simulated.
128 devices in a mesh: dp: 16 (over y, z), head: 8 (over x, core).
Axes of the slice: x: 4, y: 4, z: 4, core: 2. Of those that a mesh axis runs over, the one named last changes fastest.
Arguments:
- queries: bfloat16 [768, 128, 576], P('dp', 'head'), may hold values from -48 to 48
- kv_pool: bfloat16 [2048, 64, 576], P('dp'), may hold values from -6.1 to 6.1
- page_table: int32 [256, 8], P('dp'), may hold values from 0 to 2047, as said below
- cache_len: int32 [256], P('dp'), may hold values from 1 to 509, as said below
- accepted: int32 [256], P('dp'), may hold values from 0 to 2
- w_uv: bfloat16 [128, 512, 128], P('head'), may hold values from -0.75 to 0.75
- w_o: bfloat16 [16384, 7168], P('head', 'dp'), may hold values from -0.125 to 0.125
- residual: bfloat16 [768, 7168], P('dp'), may hold values from -6 to 6
- norm_gain: float32 [7168], replicated, may hold values from 0.5 to 1.5
- expert_ids: int32 [768, 8], P('dp'), may hold values from 0 to 15, all different within a row; in each aligned block of 48 rows (0 to 47, 48 to 95, ...) at most 32 rows name the same one
- gate_weights: float32 [768, 8], P('dp'), may hold values from 0.1 to 0.5
- w_gate: bfloat16 [16, 7168, 2048], P('dp', None, 'head'), may hold values from -0.0625 to 0.0625
- w_up: bfloat16 [16, 7168, 2048], P('dp', None, 'head'), may hold values from -0.0625 to 0.0625
- w_down: bfloat16 [16, 2048, 7168], P('dp', 'head'), may hold values from -0.125 to 0.125
Outputs:
- attended: bfloat16 [768, 7168], P('dp')
- routed: bfloat16 [768, 7168], P('dp', 'head')
Inputs may be any that keep to these rules, and one draw needn't show every extreme that they name: `page_table`: A global page number is a dp index times 128 plus one of that index's pages; no page serves two requests, and one request's pages lie on one dp index. On every dp index exactly 8 requests have their pages on other indices, each on a different one; among the indices that lend to index d are d + 1, d - 1 and d + 16 / 2 (modulo 16); every index lends to exactly 8 requests. cache_len + accepted is at most 509 for every request and equals it for some request in every draw. `expert_ids`: within the tokens of one dp index (aligned blocks of 48 rows) no expert is named more than 32 times.
All inputs are finite; a program needn't handle non-finite values.
Results may differ from a plain program's by a relative error of at most 0.035.
Values may be sent and summed in bfloat16 or wider, within the bound.
No kernel may reach another device: no remote copies, remote signals or barrier semaphores. Data moves between devices by JAX's collectives and lax.ppermute only.
A program may use at most 192 MiB of HBM per device.

v0:
```python
import jax
import jax.numpy as jnp
from jax import lax
from jax.sharding import PartitionSpec as P

LAT = 512


softmax_scale = 192.0 ** (-0.5)
norm_eps = 1e-06


def attend_rows(query_rows, key_rows, visible):
    scores = (
        jnp.einsum("njhc,npc->njhp", query_rows, key_rows, preferred_element_type=jnp.float32)
        * softmax_scale
    )
    position = jnp.arange(key_rows.shape[1], dtype=jnp.int32)
    drafts = jnp.arange(query_rows.shape[1], dtype=jnp.int32)
    allowed = (
        position[None, None, None, :] <= visible[:, None, None, None] + drafts[None, :, None, None]
    )
    highest = jnp.max(jnp.where(allowed, scores, -1e30), axis=-1, keepdims=True)
    weights = jnp.where(allowed, jnp.exp(jnp.where(allowed, scores - highest, 0.0)), 0.0)
    probs = (weights / jnp.sum(weights, axis=-1, keepdims=True)).astype(jnp.bfloat16)
    latent = jnp.einsum(
        "njhp,npc->njhc", probs, key_rows[:, :, :LAT], preferred_element_type=jnp.float32
    )
    return latent.astype(jnp.bfloat16)


def shards(
    queries,
    kv_pool,
    page_table,
    cache_len,
    accepted,
    w_uv,
    w_o,
    residual,
    norm_gain,
    expert_ids,
    gate_weights,
    w_gate,
    w_up,
    w_down,
):
    dp_count = lax.axis_size("dp")
    head_count = lax.axis_size("head")
    dp_index = lax.axis_index("dp")
    pool_pages = kv_pool.shape[0]
    page_rows = kv_pool.shape[1]
    requests = page_table.shape[0]
    span = page_table.shape[1] * page_rows
    row_width = kv_pool.shape[2]
    head_group = queries.shape[1]
    query_rows = queries.reshape(requests, 3, head_group, row_width)
    visible = cache_len + accepted
    lender = page_table[:, 0] // pool_pages
    migrated = lender != dp_index
    own_pages = jnp.where(migrated[:, None], 0, page_table - dp_index * pool_pages)
    own_keys = kv_pool[own_pages].reshape(requests, span, row_width)
    own_latent = attend_rows(query_rows, own_keys, visible)
    pair_pick = (
        (lender[None, :] == jnp.arange(dp_count, dtype=jnp.int32)[:, None]) & migrated[None, :]
    ).astype(jnp.int32)
    pick_weights = pair_pick.astype(jnp.bfloat16)
    pair_queries = jnp.einsum(
        "sr,rjhc->sjhc", pick_weights, query_rows, preferred_element_type=jnp.float32
    ).astype(jnp.bfloat16)
    pair_pages = jnp.sum(
        pair_pick[:, :, None] * (page_table - lender[:, None] * pool_pages)[None, :, :], axis=1
    )
    pair_visible = jnp.sum(pair_pick * visible[None, :], axis=1)
    fetched = lax.all_to_all(
        kv_pool[lax.all_to_all(pair_pages, "dp", split_axis=0, concat_axis=0, tiled=True)],
        "dp",
        split_axis=0,
        concat_axis=0,
        tiled=True,
    )
    pair_latent = attend_rows(
        pair_queries, fetched.reshape(dp_count, span, row_width), pair_visible
    )
    far_latent = jnp.einsum(
        "sr,sjhc->rjhc", pick_weights, pair_latent, preferred_element_type=jnp.float32
    ).astype(jnp.bfloat16)
    latent = jnp.where(migrated[:, None, None, None], far_latent, own_latent).reshape(
        requests * 3, head_group, LAT
    )
    values = jnp.einsum("thc,hcv->thv", latent, w_uv, preferred_element_type=jnp.float32).astype(
        jnp.bfloat16
    )
    values = values.reshape(requests * 3, head_group * w_uv.shape[2])
    projected = jnp.dot(
        lax.all_gather(values, "dp", axis=0, tiled=True), w_o, preferred_element_type=jnp.float32
    )
    columns = lax.all_to_all(
        projected.astype(jnp.bfloat16), "dp", split_axis=0, concat_axis=1, tiled=True
    ).astype(projected.dtype)
    attention = lax.psum(columns.astype(jnp.bfloat16), "head").astype(jnp.float32)
    attended = (residual.astype(jnp.float32) + attention).astype(jnp.bfloat16)
    wide = attended.astype(jnp.float32)
    normed = (
        wide * lax.rsqrt(jnp.mean(wide * wide, axis=-1, keepdims=True) + norm_eps) * norm_gain
    ).astype(jnp.bfloat16)
    token_rows = residual.shape[0]
    chosen_count = expert_ids.shape[1]
    local_experts = w_gate.shape[0]
    experts_all = local_experts * dp_count
    capacity = min(
        (4 * token_rows * chosen_count // (3 * experts_all) + head_count - 1)
        // head_count
        * head_count,
        token_rows // head_count * head_count,
    )
    flat_ids = expert_ids.reshape(-1)
    member = (flat_ids[:, None] == jnp.arange(experts_all, dtype=jnp.int32)[None, :]).astype(
        jnp.int32
    )
    rank = jnp.sum((jnp.cumsum(member, axis=0) - 1) * member, axis=1)
    slot_index = (flat_ids * capacity + rank).reshape(token_rows, chosen_count)
    slot_range = jnp.arange(experts_all * capacity, dtype=jnp.int32).reshape(
        dp_count, local_experts, capacity
    )
    wanted_slots = slot_range.reshape(-1)
    placing = jnp.any(slot_index[None, :, :] == wanted_slots[:, None, None], axis=2).astype(
        jnp.bfloat16
    )
    outgoing = jnp.dot(placing, normed, preferred_element_type=jnp.float32).astype(jnp.bfloat16)
    outgoing = outgoing.reshape(dp_count, local_experts * capacity, normed.shape[1])
    arrived = lax.all_to_all(outgoing, "dp", split_axis=0, concat_axis=0, tiled=True)
    incoming = arrived.reshape(dp_count, local_experts, capacity, normed.shape[1])
    gate = jnp.einsum("sxcd,xdf->sxcf", incoming, w_gate, preferred_element_type=jnp.float32)
    up = jnp.einsum("sxcd,xdf->sxcf", incoming, w_up, preferred_element_type=jnp.float32)
    hidden = (jax.nn.silu(gate) * up).astype(jnp.bfloat16)
    pieces = jnp.einsum(
        "sxcf,xfd->sxcd", hidden, w_down, preferred_element_type=jnp.float32
    ).astype(jnp.bfloat16)
    returned = lax.all_to_all(pieces, "dp", split_axis=0, concat_axis=0, tiled=True).reshape(
        experts_all * capacity, normed.shape[1]
    )
    picked = jnp.take(returned, slot_index, axis=0)
    weighted = jnp.sum(gate_weights[:, :, None] * picked.astype(jnp.float32), axis=1)
    routed = lax.psum_scatter(
        weighted.astype(jnp.bfloat16), "head", scatter_dimension=1, tiled=True
    )
    return (attended, routed)


def solution(mesh):
    return jax.shard_map(
        shards,
        mesh=mesh,
        in_specs=(
            P("dp", "head", None),
            P("dp", None, None),
            P("dp", None),
            P("dp"),
            P("dp"),
            P("head", None, None),
            P("head", "dp"),
            P("dp", None),
            P(),
            P("dp", None),
            P("dp", None),
            P("dp", None, "head"),
            P("dp", None, "head"),
            P("dp", "head", None),
        ),
        out_specs=(P("dp", None), P("dp", "head")),
        check_vma=False,
    )
```

profile of v0, /device:TPU:0, one launch (start us, length us, event | category | flops | bytes accessed | tf_op | source)
XLA Modules:
  0.0 702.7 jit_solution(13690921036011801442)
XLA Ops:
  7.2 0.8 multiply_bitcast_fusion
  8.0 0.7 broadcast_compare_fusion
  8.9 0.7 broadcast_subtract_fusion
  9.6 0.9 multiply_reduce_fusion.1
  10.5 8.1 %all-to-all-start = ((s32[16,1,8]{2,1,0:T(1,128)}), s32[16,1,8]{2,1,0:T(1,128)S(1)}, u32[]{:S(2)}, u32[]{:S(2)}) async-start(s32[16,1,8]{2,1,0:T(1,128)} %bitcast.49), calls=%async_computation | async-start | bytes 16384 | tf_op jit(solution)/shard_map/all_to_all | solution.py:76
  18.7 14.7 %copy.132 = bf16[128,64,576]{2,1,0:T(8,128)(2,1)} copy(bf16[128,64,576]{0,2,1:T(8,128)(2,1)} %param.15) | data formatting | bytes 18874368 | tf_op args[1]
  33.7 11.6 %gather_fusion = bf16[128,64,576]{2,1,0:T(8,128)(2,1)} fusion(bf16[128,64,576]{2,1,0:T(8,128)(2,1)} %copy.132, s32[1024]{0:T(1024)S(1)} %pad_clamp_fusion.2), kind=kCustom, calls=%fused_computation | custom fusion | bytes 18874880 | tf_op jit(solution)/shard_map/gather | solution.py:76
  45.3 7.3 %all-to-all-start.1 = ((bf16[16,8,64,576]{3,2,1,0:T(8,128)(2,1)}), bf16[16,8,64,576]{3,2,1,0:T(8,128)(2,1)}, u32[]{:S(2)}, u32[]{:S(2)}) async-start(bf16[16,8,64,576]{3,2,1,0:T(8,128)(2,1)} %bitcast.167), calls=%async_computation.1 | async-start | bytes 20971520 | tf_op jit(solution)/shard_map/all_to_all | solution.py:75
  52.8 11.5 %gather_fusion.1 = bf16[128,64,576]{2,1,0:T(8,128)(2,1)} fusion(bf16[128,64,576]{2,1,0:T(8,128)(2,1)} %copy.132, s32[1024]{0:T(1024)S(1)} %pad_clamp_fusion.1), kind=kCustom, calls=%fused_computation.1 | custom fusion | bytes 18874880 | tf_op jit(solution)/shard_map/gather | solution.py:62
  64.6 0.1 iota_compare_fusion.1
  64.7 0.1 iota_compare_fusion.2
  64.8 1.7 convolution_convert_fusion.2
  66.6 15.0 %fusion.76 = (f32[16,3,16]{2,1,0:T(4,128)S(1)}, f32[16,3,16,512]{3,2,1,0:T(8,128)}) fusion(pred[16,3,512]{2,1,0:T(4,128)(4,1)S(1)} %iota_compare_fusion.1, bf16[16,512,576,1]{2,1,3,0:T(8,128)(2,1)} %bitcast.168, bf16[16,3,16,576]{3,2,1,0:T(8,128)(2,1)} %bitcast.174), kind=kOutput, calls=%fused_computation.119 | convolution fusion | flops 908722688 | bytes 11922432 | tf_op jit(solution)/shard_map/sub | solution.py:24
  81.6 6.4 fusion.3
  87.9 147.5 %all-to-all-done.1 = bf16[16,8,64,576]{3,2,1,0:T(8,128)(2,1)} async-done(((bf16[16,8,64,576]{3,2,1,0:T(8,128)(2,1)}), bf16[16,8,64,576]{3,2,1,0:T(8,128)(2,1)}, u32[]{:S(2)}, u32[]{:S(2)}) %all-to-all-start.1) | async-done | bytes 9437216 | tf_op jit(solution)/shard_map/all_to_all | solution.py:75
  235.5 7.2 %convolution_multiply_fusion = f32[16,3,16,512]{3,2,1,0:T(8,128)S(1)} fusion(bf16[16,512,576,1]{2,1,3,0:T(8,128)(2,1)} %bitcast.51, bf16[16,3,16,576]{3,0,2,1:T(8,128)(2,1)S(1)} %convolution_convert_fusion.2), kind=kOutput, calls=%fused_computation.32 | convolution fusion | flops 453378048 | bytes 11894784 | tf_op jit(solution)/shard_map/njhc,npc->njhp/dot_general | solution.py:15
  242.7 8.6 %fusion.77 = (f32[16,3,16]{2,1,0:T(4,128)S(1)}, f32[16,3,16,512]{3,2,1,0:T(8,128)S(1)}) fusion(f32[16,3,16,512]{3,2,1,0:T(8,128)S(1)} %convolution_multiply_fusion, pred[16,3,512]{2,1,0:T(4,128)(4,1)S(1)} %iota_compare_fusion.2), kind=kOutput, calls=%fused_computation.120 | output fusion | flops 1966591 | bytes 3173376 | tf_op jit(solution)/shard_map/sub | solution.py:24
  251.3 5.1 fusion.18
  256.4 1.0 fusion.22
  257.4 0.4 copy.140
  257.9 1.0 fusion.38
  258.9 0.7 copy.184
  259.7 52.2 %all-gather.2.cloned.1.call-done = bf16[768,2048]{1,0:T(8,128)(2,1)} async-done(((bf16[48,2048]{1,0:T(8,128)(2,1)}), bf16[768,2048]{1,0:T(8,128)(2,1)}) %all-gather.2.cloned.1.call-update) | async-done | bytes 3145744 | tf_op jit(solution)/shard_map/all_gather | solution.py:96
  311.9 4.1 convolution_convert_fusion.4
  316.0 1.2 copy.143
  317.1 4.6 all-to-all-start.2
  322.1 0.9 reduce-window.6
  323.0 0.2 slice_reduce_fusion
  323.2 0.1 fusion.63
  323.5 12.1 %all-to-all-done.2 = bf16[16,48,448]{2,1,0:T(8,128)(2,1)S(1)} async-done(((bf16[16,48,448]{2,1,0:T(8,128)(2,1)}), bf16[16,48,448]{2,1,0:T(8,128)(2,1)S(1)}, u32[]{:S(2)}, u32[]{:S(2)}) %all-to-all-start.2) | async-done | bytes 688160 | tf_op jit(solution)/shard_map/all_to_all | solution.py:98
  335.6 0.4 copy.144
  336.0 1.8 all_to_all.38
  337.9 0.3 fusion.48
  338.2 59.0 %all-reduce.2.cloned.1.call-done = bf16[48,7168]{1,0:T(8,128)(2,1)} async-done(((bf16[48,7168]{1,0:T(8,128)(2,1)}), bf16[48,7168]{1,0:T(8,128)(2,1)}) %all-reduce.2.cloned.1.call-update) | async-done | bytes 688144 | tf_op jit(solution)/shard_map/psum | solution.py:101
  397.2 1.4 fusion.19
  398.7 2.1 convolution_convert_fusion.1
  400.8 89.3 %all_to_all.46 = bf16[16,32,7168]{2,1,0:T(8,128)(2,1)S(1)} all-to-all(bf16[16,32,7168]{2,1,0:T(8,128)(2,1)S(1)} %bitcast.166), channel_id=1, replica_groups=mesh['dp'=16,'head'=8] {'dp'}, dimensions={0} | all-to-all | bytes 14680064 | tf_op jit(solution)/shard_map/all_to_all | solution.py:132
  490.1 3.0 copy-done.2
  493.1 2.1 fusion.23
  495.2 16.0 %fusion.2 = bf16[16,1,32,7168]{3,2,1,0:T(8,128)(2,1)} fusion(bf16[1,256,7168]{2,1,0:T(8,128)(2,1)} %param.27, bf16[16,32,7168]{2,1,0:T(8,128)(2,1)} %copy-done.2, bf16[1,7168,256]{2,1,0:T(8,128)(2,1)} %param.26, f32[16,1,32,256]{3,2,0,1:T(8,128)S(1)} %fusion.23), kind=kOutput, calls=%fused_computation.8 | convolution fusion | flops 3762552832 | bytes 22544384 | tf_op jit(solution)/shard_map/sxcf,xfd->sxcd/dot_general | solution.py:137
  511.2 4.8 all-to-all-start.4
  516.3 0.1 copy.150
  516.4 88.5 %all-to-all-done.4 = bf16[16,1,32,7168]{3,2,1,0:T(8,128)(2,1)} async-done(((bf16[16,1,32,7168]{3,2,1,0:T(8,128)(2,1)}), bf16[16,1,32,7168]{3,2,1,0:T(8,128)(2,1)}, u32[]{:S(2)}, u32[]{:S(2)}) %all-to-all-start.4) | async-done | bytes 7340064 | tf_op jit(solution)/shard_map/all_to_all | solution.py:140
  605.0 17.5 %gather_fusion.2 = bf16[384,7168]{1,0:T(8,128)(2,1)} fusion(bf16[512,7168]{1,0:T(8,128)(2,1)} %bitcast.44, s32[1024]{0:T(1024)S(1)} %pad_clamp_fusion), kind=kCustom, calls=%fused_computation.2 | custom fusion | bytes 11011584 | tf_op jit(solution)/shard_map/jit(_take)/gather | solution.py:143
  622.5 8.6 %multiply_reduce_fusion = bf16[48,7168]{1,0:T(8,128)(2,1)S(1)} fusion(bf16[384,7168]{1,0:T(8,128)(2,1)} %gather_fusion.2, f32[48,8]{1,0:T(8,128)S(1)} %copy.145, pred[48,8]{1,0:T(8,128)(4,1)S(1)} %copy.150), kind=kLoop, calls=%fused_computation.5 | loop fusion | flops 10665984 | bytes 6195072 | tf_op jit(solution)/shard_map/reduce_sum | solution.py:144
  631.1 1.7 copy.167
  632.8 61.2 %reduce-scatter.4.cloned.1.call-done = bf16[896,48]{1,0:T(8,128)(2,1)} async-done(((bf16[7168,48]{1,0:T(8,128)(2,1)}), bf16[896,48]{1,0:T(8,128)(2,1)}) %reduce-scatter.4.cloned.1.call-update) | async-done | bytes 86032
  694.0 1.7 copy.168
  (60 shorter events, 1.9 us)
Async XLA Ops:
  7.2 250.7 %copy-start = (bf16[16,512,128]{2,1,0:T(8,128)(2,1)S(1)}, bf16[16,512,128]{2,1,0:T(8,128)(2,1)}, u32[]{:S(2)}) copy-start(bf16[16,512,128]{2,1,0:T(8,128)(2,1)} %param.19) | copy-start | bytes 6291460
  10.5 22.9 %all-to-all-start = ((s32[16,1,8]{2,1,0:T(1,128)}), s32[16,1,8]{2,1,0:T(1,128)S(1)}, u32[]{:S(2)}, u32[]{:S(2)}) async-start(s32[16,1,8]{2,1,0:T(1,128)} %bitcast.49), calls=%async_computation | async-start | bytes 16384 | tf_op jit(solution)/shard_map/all_to_all | solution.py:76
  45.3 190.2 %all-to-all-start.1 = ((bf16[16,8,64,576]{3,2,1,0:T(8,128)(2,1)}), bf16[16,8,64,576]{3,2,1,0:T(8,128)(2,1)}, u32[]{:S(2)}, u32[]{:S(2)}) async-start(bf16[16,8,64,576]{3,2,1,0:T(8,128)(2,1)} %bitcast.167), calls=%async_computation.1 | async-start | bytes 20971520 | tf_op jit(solution)/shard_map/all_to_all | solution.py:75
  52.6 259.3 %all-gather.2.cloned.1.call-start = ((), (), s32[]{:S(2)}) async-start(), calls=%async_computation.6 | async-start | bytes 3342336 | tf_op jit(solution)/shard_map/all_gather | solution.py:96
  52.8 11.6 %copy-start.9 = (s32[16]{0:T(128)S(1)}, s32[16]{0:T(128)}, u32[]{:S(2)}) copy-start(s32[16]{0:T(128)} %param.17) | copy-start | bytes 196
  52.8 11.6 %copy-start.10 = (s32[16]{0:T(128)S(1)}, s32[16]{0:T(128)}, u32[]{:S(2)}) copy-start(s32[16]{0:T(128)} %param.18) | copy-start | bytes 196
  251.3 5.1 copy-start.11
  259.7 62.2 %copy-start.6 = (s32[48,8]{0,1:T(8,128)S(1)}, s32[48,8]{0,1:T(8,128)}, u32[]{:S(2)}) copy-start(s32[48,8]{0,1:T(8,128)} %param.23) | copy-start | bytes 4612
  316.0 81.2 %copy-start.4 = (bf16[48,7168]{1,0:T(8,128)(2,1)S(1)}, bf16[48,7168]{1,0:T(8,128)(2,1)}, u32[]{:S(2)}) copy-start(bf16[48,7168]{1,0:T(8,128)(2,1)} %param.21) | copy-start | bytes 2064388
  317.1 81.5 %copy-start.5 = (f32[7168]{0:T(1024)S(1)}, f32[7168]{0:T(1024)}, u32[]{:S(2)}) copy-start(f32[7168]{0:T(1024)} %param.22) | copy-start | bytes 86020
  317.1 18.5 %all-to-all-start.2 = ((bf16[16,48,448]{2,1,0:T(8,128)(2,1)}), bf16[16,48,448]{2,1,0:T(8,128)(2,1)S(1)}, u32[]{:S(2)}, u32[]{:S(2)}) async-start(bf16[16,48,448]{2,1,0:T(8,128)(2,1)} %bitcast.21), calls=%async_computation.2 | async-start | bytes 1572864 | tf_op jit(solution)/shard_map/all_to_all | solution.py:98
  321.8 75.4 %all-reduce.2.cloned.1.call-start = ((), (), s32[]{:S(2)}) async-start(), calls=%async_computation.7 | async-start | bytes 1376256 | tf_op jit(solution)/shard_map/psum | solution.py:101
  398.6 2.2 copy-start.3
  400.8 92.3 %copy-start.8 = (bf16[1,7168,256]{2,1,0:T(8,128)(2,1)S(1)}, bf16[1,7168,256]{2,1,0:T(8,128)(2,1)}, u32[]{:S(2)}) copy-start(bf16[1,7168,256]{2,1,0:T(8,128)(2,1)} %param.25) | copy-start | bytes 11010052
  490.1 3.0 copy-start.2
  511.2 5.1 copy-start.7
  511.2 93.8 %all-to-all-start.4 = ((bf16[16,1,32,7168]{3,2,1,0:T(8,128)(2,1)}), bf16[16,1,32,7168]{3,2,1,0:T(8,128)(2,1)}, u32[]{:S(2)}, u32[]{:S(2)}) async-start(bf16[16,1,32,7168]{3,2,1,0:T(8,128)(2,1)} %fusion.2), calls=%async_computation.4 | async-start | bytes 14680064 | tf_op jit(solution)/shard_map/all_to_all | solution.py:140
  516.0 178.0 %reduce-scatter.4.cloned.1.call-start = ((), (), s32[]{:S(2)}) async-start(), calls=%async_computation.8 | async-start | bytes 2064384
  622.5 73.2 %copy-start.1 = (bf16[16,512,128]{2,1,0:T(8,128)(2,1)S(1)}, bf16[16,512,128]{2,1,0:T(8,128)(2,1)}, u32[]{:S(2)}) copy-start(bf16[16,512,128]{2,1,0:T(8,128)(2,1)} %param.19) | copy-start | bytes 6291460
Sparse Core Ops, SparseCore 0:
  259.8 52.0 all-gather.1
  337.9 59.2 all-reduce.1
  632.9 61.0 reduce-scatter.3
where the time goes:
time: 711 us; the launch traced here: 703 us
  waiting for transfers between devices  421 us (59%)
  blocking collectives  89.3 us (13%)
  local copies, waits for them, and re-layouts  67.8 us (10%)
  matrix products  61.7 us (9%)
  starting transfers between devices  24.9 us (4%)
  other arithmetic  23.8 us (3%)
  between operations  14.5 us (2%)
    all_to_all x1, waiting for transfers between devices, shards(): lax.all_to_all(kv_pool[lax.all_to_all(pair_pages, 'dp', split_axis=0, con...  148 us
    all_to_all x1, blocking collectives, shards(): lax.all_to_all(outgoing, 'dp', split_axis=0, concat_axis=0, tiled=True)  89.3 us
    all_to_all x1, waiting for transfers between devices, shards(): lax.all_to_all(pieces, 'dp', split_axis=0, concat_axis=0, tiled=True)  88.5 us
    unnamed x4, waiting for transfers between devices  61.3 us
    psum x1, waiting for transfers between devices, shards(): lax.psum(columns.astype(jnp.bfloat16), 'head').astype(jnp.float32)  59 us
    all_gather x1, waiting for transfers between devices, shards(): lax.all_gather(values, 'dp', axis=0, tiled=True)  52.2 us
    unnamed x29, local copies, waits for them, and re-layouts  21.3 us
    gather x1, local copies, waits for them, and re-layouts, shards(): picked = jnp.take(returned, slot_index, axis=0)  17.5 us
  transfers between devices with their start and end apart: 7, of which 6 were waited for; matrix products, arithmetic and copies ran while one was open for 7% of the time, Pallas kernels for 0%

commit v1 on v0

v1 whole, which is shorter than its diff:
```python
import jax
import jax.numpy as jnp
from jax import lax
from jax.experimental import pallas as pl
from jax.experimental.pallas import tpu as pltpu
from jax.sharding import Mesh
from jax.sharding import PartitionSpec as P

LAT = 512
DP = ("y", "z")
HEAD = ("x", "core")
ALL = ("y", "z", "x", "core")
RING = 4
DP_N = 16
HEAD_N = 8
PAGES = 128
CAP = 32

softmax_scale = 192.0 ** (-0.5)
norm_eps = 1e-06
bf16 = jnp.bfloat16
f32 = jnp.float32
i32 = jnp.int32


def hop(array, axis, step):
    return lax.ppermute(array, axis, [((i + step) % RING, i) for i in range(RING)])


def send(array, axis, step):
    return lax.ppermute(array, axis, [(i, (i + step) % RING) for i in range(RING)])


def other_core(array):
    return lax.ppermute(array, "core", [(0, 1), (1, 0)])


def pack_kernel(pick_ref, query_ref, meta_ref, out_ref):
    width = query_ref.shape[2]

    def one(i, carry):
        out_ref[i, :, :width] = query_ref[pick_ref[i]]
        out_ref[i, :, width:] = meta_ref[i]
        return carry

    lax.fori_loop(0, out_ref.shape[0], one, 0)


def pack(pick, query_rows, meta):
    count, rows, width = query_rows.shape
    return pl.pallas_call(
        pack_kernel,
        out_shape=jax.ShapeDtypeStruct((DP_N, rows, width + meta.shape[2]), bf16),
        in_specs=[
            pl.BlockSpec(memory_space=pltpu.SMEM),
            pl.BlockSpec(memory_space=pltpu.VMEM),
            pl.BlockSpec(memory_space=pltpu.VMEM),
        ],
        out_specs=pl.BlockSpec(memory_space=pltpu.VMEM),
        compiler_params=pltpu.CompilerParams(vmem_limit_bytes=32 * 2**20),
        name="pack",
    )(pick, query_rows, meta)


def attend_kernel(pick_ref, page_ref, seen_ref, own_ref, far_ref, *refs):
    pages, out_ref = refs[:-1], refs[-1]
    step = pl.program_id(0)
    width = own_ref.shape[2]
    queries = jnp.where(step < 8, own_ref[0], far_ref[0, :, :width])
    keys = jnp.concatenate([page[0] for page in pages], axis=0)
    scores = (
        lax.dot_general(queries, keys, (((1,), (1,)), ((), ())), preferred_element_type=f32)
        * softmax_scale
    )
    position = lax.broadcasted_iota(i32, scores.shape, 1)
    draft = lax.broadcasted_iota(i32, scores.shape, 0) // (scores.shape[0] // 3)
    allowed = position <= seen_ref[step] + draft
    highest = jnp.max(jnp.where(allowed, scores, -1e30), axis=-1, keepdims=True)
    weights = jnp.where(allowed, jnp.exp(jnp.where(allowed, scores - highest, 0.0)), 0.0)
    probs = (weights / jnp.sum(weights, axis=-1, keepdims=True)).astype(bf16)
    out_ref[0] = lax.dot_general(
        probs, keys[:, :LAT], (((1,), (0,)), ((), ())), preferred_element_type=f32
    ).astype(bf16)


def attend(pick, pages, seen, own_queries, far_queries, kv_pool):
    count, rows, width = own_queries.shape
    page_rows = kv_pool.shape[1]
    per = pages.shape[1]

    def page_spec(a):
        return pl.BlockSpec(
            (1, page_rows, width), lambda i, pick, page, seen: (page[i * per + a], 0, 0)
        )

    spec = pltpu.PrefetchScalarGridSpec(
        num_scalar_prefetch=3,
        grid=(count,),
        in_specs=[
            pl.BlockSpec(
                (1, rows, width), lambda i, pick, page, seen: (pick[jnp.minimum(i, 7)], 0, 0)
            ),
            pl.BlockSpec(
                (1, rows, far_queries.shape[2]),
                lambda i, pick, page, seen: (pick[jnp.maximum(i, 8)], 0, 0),
            ),
        ]
        + [page_spec(a) for a in range(per)],
        out_specs=pl.BlockSpec((1, rows, LAT), lambda i, pick, page, seen: (i, 0, 0)),
    )
    return pl.pallas_call(
        attend_kernel,
        out_shape=jax.ShapeDtypeStruct((count, rows, LAT), bf16),
        grid_spec=spec,
        compiler_params=pltpu.CompilerParams(vmem_limit_bytes=32 * 2**20),
        cost_estimate=pl.CostEstimate(
            flops=count * rows * 512 * 1088 * 2, bytes_accessed=12_000_000, transcendentals=0
        ),
        name="attend",
    )(pick, pages.reshape(-1), seen, own_queries, far_queries, *([kv_pool] * per))


def before(count):
    at = jnp.arange(count, dtype=i32)
    return at[:, None] < at[None, :]


def shards(
    queries,
    kv_pool,
    page_table,
    cache_len,
    accepted,
    w_uv,
    w_o,
    residual,
    norm_gain,
    expert_ids,
    gate_weights,
    w_gate,
    w_up,
    w_down,
):
    at_x, at_y, at_z = lax.axis_index("x"), lax.axis_index("y"), lax.axis_index("z")
    at_core = lax.axis_index("core")
    dp_index = at_y * RING + at_z
    requests = page_table.shape[0]
    tokens, head_group, width = queries.shape
    query_rows = queries.reshape(requests, 3 * head_group, width)
    visible = cache_len + accepted
    lender = page_table[:, 0] // PAGES
    far = lender != dp_index
    dps = jnp.arange(DP_N, dtype=i32)

    lent_to = ((lender[None, :] == dps[:, None]) & far[None, :]).astype(i32)
    pick = jnp.sum(lent_to * jnp.arange(requests, dtype=i32)[None, :], axis=1)
    sent_pages = jnp.sum(lent_to[:, :, None] * (page_table - lender[:, None] * PAGES)[None], axis=1)
    sent_seen = jnp.sum(lent_to * visible[None, :], axis=1)
    sent_any = jnp.sum(lent_to, axis=1)
    line0 = jnp.concatenate(
        [
            sent_pages,
            (sent_seen // 2)[:, None],
            (sent_seen % 2)[:, None],
            sent_any[:, None],
            jnp.zeros((DP_N, 5), i32),
            jnp.broadcast_to(lender[None, :], (DP_N, requests)),
        ],
        axis=1,
    )
    ids_block = jnp.pad(expert_ids, ((0, 0), (0, 56)))
    line_block = jnp.pad(line0[:, None, :], ((0, 0), (0, tokens - 1), (8, 24)))
    meta = (ids_block[None] + line_block).astype(bf16)
    arrived = lax.all_to_all(pack(pick, query_rows, meta), DP, 0, 0, tiled=True)
    told = arrived[:, :, width:].astype(i32)
    all_ids = told[:, :, :8]
    told_pages = told[:, 0, 8:16]
    told_seen = told[:, 0, 16] * 2 + told[:, 0, 17]
    told_any = told[:, 0, 18]
    lenders = told[:, 0, 24:40]

    slots = jnp.arange(8, dtype=i32)
    own = 1 - far.astype(i32)
    own_rank = jnp.sum(before(requests) * own[:, None], axis=0)
    own_pick = ((own_rank[None, :] == slots[:, None]) & (own[None, :] > 0)).astype(i32)
    far_rank = jnp.sum(before(DP_N) * told_any[:, None], axis=0)
    far_pick = ((far_rank[None, :] == slots[:, None]) & (told_any[None, :] > 0)).astype(i32)
    which = jnp.concatenate([jnp.sum(own_pick * dps, axis=1), jnp.sum(far_pick * dps, axis=1)])
    held_pages = jnp.concatenate(
        [
            jnp.sum(own_pick[:, :, None] * (page_table - dp_index * PAGES)[None], axis=1),
            jnp.sum(far_pick[:, :, None] * told_pages[None], axis=1),
        ]
    )
    held_seen = jnp.concatenate(
        [jnp.sum(own_pick * visible, axis=1), jnp.sum(far_pick * told_seen, axis=1)]
    )
    latent = attend(which, held_pages, held_seen, query_rows, arrived, kv_pool)
    values = jnp.einsum(
        "thc,hcv->thv",
        latent.reshape(tokens, head_group, LAT),
        w_uv,
        preferred_element_type=f32,
    ).astype(bf16)
    values = values.reshape(tokens, head_group * w_uv.shape[2])

    half = values.shape[1] // 2

    def spread(block, first, second):
        line = jnp.concatenate([block] + [hop(block, first, k) for k in (1, 2, 3)], axis=0)
        return [line] + [hop(line, second, k) for k in (1, 2, 3)]

    zy = spread(values[:, :half], "z", "y")
    yz = spread(values[:, half:], "y", "z")
    part_zy = jnp.concatenate(
        [jnp.dot(a, w_o[:half], preferred_element_type=f32) for a in zy], axis=0
    )
    part_yz = jnp.concatenate(
        [jnp.dot(a, w_o[half:], preferred_element_type=f32) for a in yz], axis=0
    )
    columns = w_o.shape[1]
    part_yz = part_yz.reshape(RING, RING, tokens, columns).transpose(1, 0, 2, 3)
    projected = (part_zy + part_yz.reshape(-1, columns)).astype(bf16)

    is_own = (lenders == dps[:, None]).astype(i32)
    own_slot = jnp.sum(is_own[:, :, None] * before(requests)[None], axis=1)
    at_lender = (lenders[:, :, None] == dps[None, None, :]).astype(i32)
    away = at_lender * (dps[:, None, None] != dps[None, None, :])
    lends = jnp.sum(away, axis=1)
    lend_rank = jnp.sum(before(DP_N)[:, :, None] * lends[:, None, :], axis=0)
    far_slot = 8 + jnp.sum(at_lender * lend_rank[:, None, :], axis=2)
    slot = jnp.where(is_own > 0, own_slot, far_slot)
    turned = ((lenders // RING - at_y) % RING) * RING + (lenders % RING - at_z) % RING
    first_row = (turned * requests + slot) * 3
    source = (first_row[:, :, None] + jnp.arange(3, dtype=i32)).reshape(DP_N, RING, 2, -1)
    source = source.transpose(1, 2, 0, 3).reshape(RING, 2, -1)
    source = lax.dynamic_slice_in_dim(jnp.concatenate([source, source], 0), at_x, RING, 0)
    source = lax.dynamic_slice_in_dim(jnp.concatenate([source, source], 1), at_core, 2, 1)
    source = source.transpose(1, 0, 2).reshape(-1)
    rows_all = projected.shape[0]
    moves = (source[:, None] == jnp.arange(rows_all, dtype=i32)[None, :]).astype(bf16)
    homed = jnp.dot(moves, projected, preferred_element_type=f32)
    kept = homed[: rows_all // 2] + other_core(homed[rows_all // 2 :].astype(bf16)).astype(f32)
    kept = kept.reshape(RING, -1, columns)
    mine = kept[0]
    for k in (1, 2, 3):
        mine = mine + send(kept[k].astype(bf16), "x", k).astype(f32)
    share = tokens // HEAD_N
    mine = lax.all_to_all(
        mine.astype(bf16).reshape(DP_N, share, columns), DP, 0, 0, tiled=True
    )
    attention = mine.transpose(1, 0, 2).reshape(share, DP_N * columns)
    head_index = at_x * 2 + at_core
    near = lax.dynamic_slice_in_dim(residual, head_index * share, share, 0)
    attended_part = (near.astype(f32) + attention.astype(f32)).astype(bf16)
    wide = attended_part.astype(f32)
    normed = (
        wide * lax.rsqrt(jnp.mean(wide * wide, axis=-1, keepdims=True) + norm_eps) * norm_gain
    ).astype(bf16)
    padded = 8
    fill = ((0, padded - share), (0, 0))
    attended = lax.all_gather(jnp.pad(attended_part, fill), HEAD, axis=0, tiled=True)
    attended = attended.reshape(HEAD_N, padded, -1)[:, :share].reshape(tokens, -1)
    rows = lax.all_gather(jnp.pad(normed, fill), ALL, axis=0, tiled=True)

    gate = jnp.dot(rows, w_gate[0], preferred_element_type=f32)
    up = jnp.dot(rows, w_up[0], preferred_element_type=f32)
    hidden = (jax.nn.silu(gate) * up).astype(bf16)
    member = jnp.sum((all_ids == dp_index).astype(i32), axis=2)
    rank = jnp.sum(before(tokens)[None] * member[:, :, None], axis=1)
    place = jnp.where(member > 0, dps[:, None] * CAP + rank, -1)
    place = jnp.pad(
        place.reshape(DP_N, HEAD_N, share), ((0, 0), (0, 0), (0, padded - share)), constant_values=-1
    ).reshape(-1)
    slots_all = jnp.arange(DP_N * CAP, dtype=i32)
    placing = (slots_all[:, None] == place[None, :]).astype(bf16)
    hidden = jnp.dot(placing, hidden, preferred_element_type=f32).astype(bf16)
    width_out = w_down.shape[2] // HEAD_N
    down = w_down[0].reshape(-1, RING, 2, width_out)

    def piece(k, core):
        block = lax.dynamic_slice_in_dim(down, (at_x + k) % RING, 1, 1)
        block = lax.dynamic_slice_in_dim(block, core, 1, 2)
        return jnp.dot(hidden, block.reshape(-1, width_out), preferred_element_type=f32)

    total = None
    for k in (2, 1, 3, 0):
        there = other_core(piece(k, 1 - at_core).astype(bf16))
        both = piece(k, at_core) + there.astype(f32)
        if k:
            both = send(both.astype(bf16), "x", k).astype(f32)
        total = both if total is None else total + both
    total = total.astype(bf16).reshape(DP_N, CAP, width_out)
    returned = lax.all_to_all(total, DP, 0, 0, tiled=True).reshape(DP_N * CAP, width_out)
    chosen = (expert_ids[:, :, None] == dps[None, None, :]).astype(i32)
    named = jnp.sum(chosen, axis=1)
    weight = jnp.sum(chosen.astype(f32) * gate_weights[:, :, None], axis=1)
    my_rank = jnp.sum(before(tokens)[:, :, None] * named[:, None, :], axis=0)
    ranks = jnp.arange(CAP, dtype=i32)
    mix = jnp.where(my_rank[:, :, None] == ranks[None, None, :], weight[:, :, None], 0.0)
    mix = mix.reshape(tokens, DP_N * CAP)
    high = lax.reduce_precision(mix, 8, 7)
    both = jnp.concatenate([high.astype(bf16), (mix - high).astype(bf16)], axis=0)
    routed = jnp.dot(both, returned, preferred_element_type=f32)
    routed = (routed[:tokens] + routed[tokens:]).astype(bf16)
    return (attended, routed)


def solution(mesh):
    grid = Mesh(mesh.devices.reshape(RING, RING, RING, 2), ALL)
    return jax.shard_map(
        shards,
        mesh=grid,
        in_specs=(
            P(DP, HEAD, None),
            P(DP, None, None),
            P(DP, None),
            P(DP),
            P(DP),
            P(HEAD, None, None),
            P(HEAD, DP),
            P(DP, None),
            P(),
            P(DP, None),
            P(DP, None),
            P(DP, None, HEAD),
            P(DP, None, HEAD),
            P(DP, HEAD, None),
        ),
        out_specs=(P(DP, None), P(DP, HEAD)),
        check_vma=False,
    )
```

time: 711 us -> 317 us (0.45)
  waiting for transfers between devices: 421 us -> 122 us
  blocking collectives: 89.3 us -> 14.7 us
  starting transfers between devices: 24.9 us -> 56.7 us
  local copies, waits for them, and re-layouts: 67.8 us -> 36.7 us
  matrix products: 61.7 us -> 44.6 us
  Pallas kernels: 0 us -> 12.8 us
  other arithmetic: 23.8 us -> 12 us
    all_to_all x4 -> x3, waiting for transfers between devices: 248 us -> 9.67 us  [the longest x1 7.78 us: shards(): lax.all_to_all(mine.astype(bf16).reshape(DP_N, share, columns), DP, 0, 0,...]
    all_to_all x1 -> x0, blocking collectives: 89.3 us -> none  [shards(): lax.all_to_all(outgoing, 'dp', split_axis=0, concat_axis=0, tiled=True)]
    unnamed x4 -> x1, waiting for transfers between devices: 61.3 us -> 0.02 us
    psum x1 -> x0, waiting for transfers between devices: 59 us -> none  [shards(): lax.psum(columns.astype(jnp.bfloat16), 'head').astype(jnp.float32)]
    ppermute x0 -> x23, waiting for transfers between devices: none -> 44.5 us  [the longest x6 35 us: send(): lax.ppermute(array, axis, [(i, (i + step) % RING) for i in range(RING)])]
    gather x3 -> x0, local copies, waits for them, and re-layouts: 40.6 us -> none  [the longest x1 17.5 us: shards(): picked = jnp.take(returned, slot_index, axis=0)]
    ppermute x0 -> x23, starting transfers between devices: none -> 32.7 us  [the longest x12 19.5 us: hop(): lax.ppermute(array, axis, [((i + step) % RING, i) for i in range(RING)])]
    all_gather x1, waiting for transfers between devices: 52.2 us -> 67.8 us  [shards(): rows = lax.all_gather(jnp.pad(normed, fill), ALL, axis=0, tiled=True)]
  transfers between devices with their start and end apart: 7 -> 27, of which waited for: 6 -> 13; matrix products, arithmetic and copies ran while one was open for 7% -> 15% of each run, Pallas kernels for 0% -> 0%
where the time goes in v1:
time: 317 us; the launch traced here: 314 us
  waiting for transfers between devices  122 us (38%)
  starting transfers between devices  56.7 us (18%)
  matrix products  44.6 us (14%)
  local copies, waits for them, and re-layouts  36.7 us (12%)
  blocking collectives  14.7 us (5%)
  between operations  14.7 us (5%)
  Pallas kernels  12.8 us (4%)
  other arithmetic  12 us (4%)
    all_gather x1, waiting for transfers between devices, shards(): rows = lax.all_gather(jnp.pad(normed, fill), ALL, axis=0, tiled=True)  67.8 us
    ppermute x6, waiting for transfers between devices, send(): lax.ppermute(array, axis, [(i, (i + step) % RING) for i in range(RING)])  35 us
    unnamed x29, local copies, waits for them, and re-layouts  29.1 us
    ppermute x12, starting transfers between devices, hop(): lax.ppermute(array, axis, [((i + step) % RING, i) for i in range(RING)])  19.5 us
    dot_general x8, matrix products, piece(): jnp.dot(hidden, block.reshape(-1, width_out), preferred_element_type=f32)  18.2 us
    all_gather x1, blocking collectives, shards(): lax.all_gather(jnp.pad(attended_part, fill), HEAD, axis=0, tiled=True)  14.7 us
    ppermute x6, starting transfers between devices, send(): lax.ppermute(array, axis, [(i, (i + step) % RING) for i in range(RING)])  11.9 us
    pallas_call x1, Pallas kernels, attend(): pl.pallas_call(attend_kernel, out_shape=jax.ShapeDtypeStruct((count, rows...  11.1 us
  transfers between devices with their start and end apart: 27, of which 13 were waited for; matrix products, arithmetic and copies ran while one was open for 15% of the time, Pallas kernels for 0%

profile of v1, /device:TPU:0, one launch (start us, length us, event | category | flops | bytes accessed | tf_op | source)
XLA Modules:
  0.0 314.2 jit_solution(8799934276839883051)
XLA Ops:
  12.0 1.2 copy-done.3
  13.2 1.7 pack.1
  15.9 8.1 %all-to-all-start = ((bf16[16,48,640]{2,1,0:T(8,128)(2,1)}), bf16[16,48,640]{2,1,0:T(8,128)(2,1)S(1)}, u32[]{:S(2)}, u32[]{:S(2)}) async-start(bf16[16,48,640]{2,1,0:T(8,128)(2,1)} %copy-done.5), calls=%async_computation | async-start | bytes 1966080 | tf_op jit(solution)/shard_map/all_to_all | solution.py:174
  24.1 14.8 %copy.165.refs_0_.refs_1_.refs_2_.refs_3_.refs_4_.refs_5_.refs_6_.refs_7_ = bf16[128,64,576]{2,1,0:T(8,128)(2,1)} copy(bf16[128,64,576]{0,2,1:T(8,128)(2,1)} %param.15) | data formatting | bytes 18874368 | tf_op args[1]
  39.0 1.9 all-to-all-done.far_ref
  42.8 4.0 %copy-done.2 = bf16[128,64,576]{2,1,0:T(8,128)(2,1)S(1)} copy-done((bf16[128,64,576]{2,1,0:T(8,128)(2,1)S(1)}, bf16[128,64,576]{2,1,0:T(8,128)(2,1)}, u32[]{:S(2)}) %copy-start.2) | copy-done | bytes 9437208
  46.8 1.2 copy-done.4
  48.0 11.1 %attend.1 = bf16[16,48,512]{2,1,0:T(8,128)(2,1)S(1)} custom-call(s32[16]{0:T(128)S(1)} %pad_add_fusion.1.pick_ref, s32[128]{0:T(128)S(1)} %reshape.538.page_ref, s32[16]{0:T(128)S(1)} %pad_add_fusion.2.seen_ref, bf16[16,48,576]{2,1,0:T(8,128)(2,1)S(1)} %bitcast.116, bf16[16,48,640]{2,1,0:T(8,128)(2,1)S(1)} %all-to-all-done.far_ref, ...), custom_call_target="tpu_custom_call" | custom-call | flops 855638016 | bytes 12000000 | tf_op jit(solution)/shard_map/attend/pallas_call | solution.py:111
  59.1 1.1 fusion.15
  60.3 1.3 collective-permute-start.6
  63.4 2.7 collective-permute-start
  69.2 1.8 collective-permute-start.11
  71.0 2.2 collective-permute-start.10
  73.2 1.5 collective-permute-start.9
  75.3 1.8 collective-permute-start.5
  77.1 2.1 collective-permute-start.4
  79.2 1.6 fusion.24
  81.3 1.8 collective-permute-done.11
  83.1 2.7 collective-permute-start.3
  86.2 3.8 %collective-permute-done.10 = bf16[192,1024]{1,0:T(8,128)(2,1)S(1)} collective-permute-done((bf16[192,1024]{1,0:T(8,128)(2,1)S(1)}, bf16[192,1024]{1,0:T(8,128)(2,1)S(1)}, u32[]{:S(2)}, u32[]{:S(2)}) %collective-permute-start.10) | collective-permute-done | bytes 393248 | tf_op jit(solution)/shard_map/ppermute | solution.py:27
  91.0 1.7 collective-permute-done.5
  95.8 1.6 collective-permute-done.12
  97.7 1.6 collective-permute-start.13
  99.3 2.7 collective-permute-start.14
  102.0 1.4 collective-permute-start.15
  104.2 3.4 %collective-permute-done.14 = bf16[96,448]{0,1:T(8,128)(2,1)S(1)} collective-permute-done((bf16[96,448]{0,1:T(8,128)(2,1)S(1)}, bf16[96,448]{0,1:T(8,128)(2,1)S(1)}, u32[]{:S(2)}, u32[]{:S(2)}) %collective-permute-start.14) | collective-permute-done | bytes 86048 | tf_op jit(solution)/shard_map/ppermute | solution.py:31
  108.5 9.8 %all-to-all-start.1 = ((bf16[16,6,448]{2,1,0:T(8,128)(2,1)}), bf16[16,6,448]{2,1,0:T(8,128)(2,1)S(1)}, u32[]{:S(2)}, u32[]{:S(2)}) async-start(bf16[16,6,448]{2,1,0:T(8,128)(2,1)} %reshape.543), calls=%async_computation.1 | async-start | bytes 262144 | tf_op jit(solution)/shard_map/all_to_all | solution.py:249
  118.3 7.8 %all-to-all-done.1 = bf16[16,6,448]{2,1,0:T(8,128)(2,1)S(1)} async-done(((bf16[16,6,448]{2,1,0:T(8,128)(2,1)}), bf16[16,6,448]{2,1,0:T(8,128)(2,1)S(1)}, u32[]{:S(2)}, u32[]{:S(2)}) %all-to-all-start.1) | async-done | bytes 86048 | tf_op jit(solution)/shard_map/all_to_all | solution.py:249
  128.4 5.9 %copy.184 = bf16[1,256,7168]{1,2,0:T(8,128)(2,1)} copy(bf16[1,256,7168]{2,1,0:T(8,128)(2,1)} %param.27) | data formatting | bytes 7340032 | tf_op args[13]
  135.3 67.8 %all-gather.2.cloned.1.call-done = bf16[1024,7168]{1,0:T(8,128)(2,1)} async-done(((bf16[8,7168]{1,0:T(8,128)(2,1)}), bf16[1024,7168]{1,0:T(8,128)(2,1)}) %all-gather.2.cloned.1.call-update) | async-done | bytes 14680080 | tf_op jit(solution)/shard_map/all_gather | solution.py:264
  203.2 8.3 %fusion.2 = f32[1024,256]{1,0:T(8,128)S(1)} fusion(bf16[1024,7168]{1,0:T(8,128)(2,1)} %all-gather.2.cloned.1.call-done, bf16[1,7168,256]{2,1,0:T(8,128)(2,1)} %param.25), kind=kOutput, calls=%fused_computation.2 | convolution fusion | flops 3758096384 | bytes 19398656 | tf_op jit(solution)/shard_map/dot_general | solution.py:266
  211.5 11.0 %fusion.13 = bf16[512,256]{1,0:T(8,128)(2,1)S(1)} fusion(s32[1024]{0:T(1024)S(1)} %eq.202, bf16[1024,7168]{1,0:T(8,128)(2,1)} %all-gather.2.cloned.1.call-done, bf16[1,7168,256]{2,1,0:T(8,128)(2,1)} %param.26, f32[1024,256]{1,0:T(8,128)S(1)} %fusion.2), kind=kOutput, calls=%fused_computation.21 | convolution fusion | flops 4028760064 | bytes 19664896 | tf_op jit(solution)/shard_map/dot_general | solution.py:277
  222.4 1.5 convolution_convert_fusion.3
  224.3 2.4 convolution_convert_fusion.2
  226.9 2.4 convolution_convert_fusion.1
  229.7 2.5 convolution_convert_fusion
  232.4 2.4 add_convert_fusion.3
  234.8 3.0 collective-permute-start.17
  237.8 2.7 add_convert_fusion.2
  241.1 2.8 add_convert_fusion.1
  243.8 2.7 collective-permute-start.21
  246.6 1.5 fusion.35
  248.1 11.7 %collective-permute-done.17 = bf16[512,896]{1,0:T(8,128)(2,1)} collective-permute-done((bf16[512,896]{1,0:T(8,128)(2,1)}, bf16[512,896]{1,0:T(8,128)(2,1)}, u32[]{:S(2)}, u32[]{:S(2)}) %collective-permute-start.17) | collective-permute-done | bytes 917536 | tf_op jit(solution)/shard_map/ppermute | solution.py:31
  259.8 19.0 %collective-permute-done.19 = bf16[512,896]{1,0:T(8,128)(2,1)} collective-permute-done((bf16[512,896]{1,0:T(8,128)(2,1)}, bf16[512,896]{1,0:T(8,128)(2,1)}, u32[]{:S(2)}, u32[]{:S(2)}) %collective-permute-start.19) | collective-permute-done | bytes 917536 | tf_op jit(solution)/shard_map/ppermute | solution.py:31
  278.9 3.2 %add_convert_fusion = bf16[512,896]{1,0:T(8,128)(2,1)} fusion(f32[512,896]{1,0:T(8,128)S(1)} %fusion.35, bf16[512,896]{1,0:T(8,128)(2,1)S(1)} %collective-permute-done.22, bf16[512,896]{1,0:T(8,128)(2,1)} %collective-permute-done.21, bf16[512,896]{1,0:T(8,128)(2,1)} %collective-permute-done.19, bf16[512,896]{1,0:T(8,128)(2,1)} %collective-permute-done.17), kind=kLoop, calls=%fused_computation.8 | loop fusion | flops 4128768 | bytes 6422528 | tf_op jit(solution)/shard_map/convert_element_type | solution.py:293
  282.1 6.1 %all-to-all-start.2 = ((bf16[16,32,896]{2,1,0:T(8,128)(2,1)}), bf16[16,32,896]{2,1,0:T(8,128)(2,1)S(1)}, u32[]{:S(2)}, u32[]{:S(2)}) async-start(bf16[16,32,896]{2,1,0:T(8,128)(2,1)} %bitcast.26), calls=%async_computation.2 | async-start | bytes 1835008 | tf_op jit(solution)/shard_map/all_to_all | solution.py:294
  289.4 14.7 %all_gather.6 = bf16[64,7168]{1,0:T(8,128)(2,1)} all-gather(bf16[8,7168]{1,0:T(8,128)(2,1)S(1)} %pad.21), channel_id=1, replica_groups=mesh['y'=4,'z'=4,'x'=4,'core'=2] {'x','core'}, dimensions={0}, use_global_device_ids=true | all-gather | bytes 1032192 | tf_op jit(solution)/shard_map/all_gather | solution.py:262
  304.1 2.3 reshape.545
  (160 shorter events, 27.2 us)
Async XLA Ops:
  7.2 51.9 %copy-start = (bf16[16,512,128]{2,1,0:T(8,128)(2,1)S(1)}, bf16[16,512,128]{2,1,0:T(8,128)(2,1)}, u32[]{:S(2)}) copy-start(bf16[16,512,128]{2,1,0:T(8,128)(2,1)} %param.19) | copy-start | bytes 6291460
  12.0 1.2 copy-start.3
  15.0 1.0 copy-start.5
  15.9 25.0 %all-to-all-start = ((bf16[16,48,640]{2,1,0:T(8,128)(2,1)}), bf16[16,48,640]{2,1,0:T(8,128)(2,1)S(1)}, u32[]{:S(2)}, u32[]{:S(2)}) async-start(bf16[16,48,640]{2,1,0:T(8,128)(2,1)} %copy-done.5), calls=%async_computation | async-start | bytes 1966080 | tf_op jit(solution)/shard_map/all_to_all | solution.py:174
  42.8 4.0 %copy-start.2 = (bf16[128,64,576]{2,1,0:T(8,128)(2,1)S(1)}, bf16[128,64,576]{2,1,0:T(8,128)(2,1)}, u32[]{:S(2)}) copy-start(bf16[128,64,576]{2,1,0:T(8,128)(2,1)} %copy.165.refs_0_.refs_1_.refs_2_.refs_3_.refs_4_.refs_5_.refs_6_.refs_7_) | copy-start | bytes 28311556
  46.8 1.2 copy-start.4
  60.3 7.9 %collective-permute-start.6 = (bf16[48,1024]{1,0:T(8,128)(2,1)S(1)}, bf16[48,1024]{1,0:T(8,128)(2,1)S(1)}, u32[]{:S(2)}, u32[]{:S(2)}) collective-permute-start(bf16[48,1024]{1,0:T(8,128)(2,1)S(1)} %get-tuple-element.27), channel_id=1, source_target_pairs={{32,0},{64,32},{96,64},{0,96},{33,1},{65,33},{97,65},{1,97},{34,2}... | collective-permute-start | bytes 294920 | tf_op jit(solution)/shard_map/ppermute | solution.py:27
  61.6 7.5 %collective-permute-start.7 = (bf16[48,1024]{1,0:T(8,128)(2,1)S(1)}, bf16[48,1024]{1,0:T(8,128)(2,1)S(1)}, u32[]{:S(2)}, u32[]{:S(2)}) collective-permute-start(bf16[48,1024]{1,0:T(8,128)(2,1)S(1)} %get-tuple-element.27), channel_id=1, source_target_pairs={{64,0},{96,32},{0,64},{32,96},{65,1},{97,33},{1,65},{33,97},{66,2}... | collective-permute-start | bytes 294920 | tf_op jit(solution)/shard_map/ppermute | solution.py:27
  62.5 6.6 %collective-permute-start.8 = (bf16[48,1024]{1,0:T(8,128)(2,1)S(1)}, bf16[48,1024]{1,0:T(8,128)(2,1)S(1)}, u32[]{:S(2)}, u32[]{:S(2)}) collective-permute-start(bf16[48,1024]{1,0:T(8,128)(2,1)S(1)} %get-tuple-element.27), channel_id=1, source_target_pairs={{96,0},{0,32},{32,64},{64,96},{97,1},{1,33},{33,65},{65,97},{98,2}... | collective-permute-start | bytes 294920 | tf_op jit(solution)/shard_map/ppermute | solution.py:27
  63.4 9.8 %collective-permute-start = (bf16[48,1024]{1,0:T(8,128)(2,1)S(1)}, bf16[48,1024]{1,0:T(8,128)(2,1)S(1)}, u32[]{:S(2)}, u32[]{:S(2)}) collective-permute-start(bf16[48,1024]{1,0:T(8,128)(2,1)S(1)} %get-tuple-element.28), channel_id=1, source_target_pairs={{8,0},{16,8},{24,16},{0,24},{9,1},{17,9},{25,17},{1,25},{10,2},{18... | collective-permute-start | bytes 294920 | tf_op jit(solution)/shard_map/ppermute | solution.py:27
  66.0 8.6 %collective-permute-start.1 = (bf16[48,1024]{1,0:T(8,128)(2,1)S(1)}, bf16[48,1024]{1,0:T(8,128)(2,1)S(1)}, u32[]{:S(2)}, u32[]{:S(2)}) collective-permute-start(bf16[48,1024]{1,0:T(8,128)(2,1)S(1)} %get-tuple-element.28), channel_id=1, source_target_pairs={{16,0},{24,8},{0,16},{8,24},{17,1},{25,9},{1,17},{9,25},{18,2},{26... | collective-permute-start | bytes 294920 | tf_op jit(solution)/shard_map/ppermute | solution.py:27
  68.3 7.0 %collective-permute-start.2 = (bf16[48,1024]{1,0:T(8,128)(2,1)S(1)}, bf16[48,1024]{1,0:T(8,128)(2,1)S(1)}, u32[]{:S(2)}, u32[]{:S(2)}) collective-permute-start(bf16[48,1024]{1,0:T(8,128)(2,1)S(1)} %get-tuple-element.28), channel_id=1, source_target_pairs={{24,0},{0,8},{8,16},{16,24},{25,1},{1,9},{9,17},{17,25},{26,2},{2,... | collective-permute-start | bytes 294920 | tf_op jit(solution)/shard_map/ppermute | solution.py:27
  69.2 11.6 %copy-start.11 = (bf16[2048,448]{0,1:T(8,128)(2,1)S(1)}, bf16[2048,448]{0,1:T(8,128)(2,1)}, u32[]{:S(2)}) copy-start(bf16[2048,448]{0,1:T(8,128)(2,1)} %param.20) | copy-start | bytes 5505028
  69.2 13.9 %collective-permute-start.11 = (bf16[192,1024]{1,0:T(8,128)(2,1)S(1)}, bf16[192,1024]{1,0:T(8,128)(2,1)S(1)}, u32[]{:S(2)}, u32[]{:S(2)}) collective-permute-start(bf16[192,1024]{1,0:T(8,128)(2,1)S(1)} %pad_maximum_fusion.2), channel_id=1, source_target_pairs={{24,0},{0,8},{8,16},{16,24},{25,1},{1,9},{9,17},{17,25},{26,2},{2,... | collective-permute-start | bytes 1179656 | tf_op jit(solution)/shard_map/ppermute | solution.py:27
  71.0 19.0 %collective-permute-start.10 = (bf16[192,1024]{1,0:T(8,128)(2,1)S(1)}, bf16[192,1024]{1,0:T(8,128)(2,1)S(1)}, u32[]{:S(2)}, u32[]{:S(2)}) collective-permute-start(bf16[192,1024]{1,0:T(8,128)(2,1)S(1)} %pad_maximum_fusion.2), channel_id=1, source_target_pairs={{16,0},{24,8},{0,16},{8,24},{17,1},{25,9},{1,17},{9,25},{18,2},{26... | collective-permute-start | bytes 1179656 | tf_op jit(solution)/shard_map/ppermute | solution.py:27
  73.2 17.3 %collective-permute-start.9 = (bf16[192,1024]{1,0:T(8,128)(2,1)S(1)}, bf16[192,1024]{1,0:T(8,128)(2,1)S(1)}, u32[]{:S(2)}, u32[]{:S(2)}) collective-permute-start(bf16[192,1024]{1,0:T(8,128)(2,1)S(1)} %pad_maximum_fusion.2), channel_id=1, source_target_pairs={{8,0},{16,8},{24,16},{0,24},{9,1},{17,9},{25,17},{1,25},{10,2},{18... | collective-permute-start | bytes 1179656 | tf_op jit(solution)/shard_map/ppermute | solution.py:27
  75.3 17.4 %collective-permute-start.5 = (bf16[192,1024]{1,0:T(8,128)(2,1)S(1)}, bf16[192,1024]{1,0:T(8,128)(2,1)S(1)}, u32[]{:S(2)}, u32[]{:S(2)}) collective-permute-start(bf16[192,1024]{1,0:T(8,128)(2,1)S(1)} %pad_maximum_fusion.1), channel_id=1, source_target_pairs={{96,0},{0,32},{32,64},{64,96},{97,1},{1,33},{33,65},{65,97},{98,2}... | collective-permute-start | bytes 1179656 | tf_op jit(solution)/shard_map/ppermute | solution.py:27
  77.1 16.3 %collective-permute-start.4 = (bf16[192,1024]{1,0:T(8,128)(2,1)S(1)}, bf16[192,1024]{1,0:T(8,128)(2,1)S(1)}, u32[]{:S(2)}, u32[]{:S(2)}) collective-permute-start(bf16[192,1024]{1,0:T(8,128)(2,1)S(1)} %pad_maximum_fusion.1), channel_id=1, source_target_pairs={{64,0},{96,32},{0,64},{32,96},{65,1},{97,33},{1,65},{33,97},{66,2}... | collective-permute-start | bytes 1179656 | tf_op jit(solution)/shard_map/ppermute | solution.py:27
  83.1 10.8 %collective-permute-start.3 = (bf16[192,1024]{1,0:T(8,128)(2,1)S(1)}, bf16[192,1024]{1,0:T(8,128)(2,1)S(1)}, u32[]{:S(2)}, u32[]{:S(2)}) collective-permute-start(bf16[192,1024]{1,0:T(8,128)(2,1)S(1)} %pad_maximum_fusion.1), channel_id=1, source_target_pairs={{32,0},{64,32},{96,64},{0,96},{33,1},{65,33},{97,65},{1,97},{34,2}... | collective-permute-start | bytes 1179656 | tf_op jit(solution)/shard_map/ppermute | solution.py:27
  95.7 1.7 collective-permute-start.12
  97.5 30.0 %copy-start.9 = (f32[7168]{0:T(1024)S(1)}, f32[7168]{0:T(1024)}, u32[]{:S(2)}) copy-start(f32[7168]{0:T(1024)} %param.22) | copy-start | bytes 86020
  97.7 6.5 %collective-permute-start.13 = (bf16[96,448]{0,1:T(8,128)(2,1)S(1)}, bf16[96,448]{0,1:T(8,128)(2,1)S(1)}, u32[]{:S(2)}, u32[]{:S(2)}) collective-permute-start(bf16[96,448]{0,1:T(8,128)(2,1)S(1)} %get-tuple-element.22), channel_id=1, source_target_pairs={{0,2},{2,4},{4,6},{6,0},{1,3},{3,5},{5,7},{7,1},{8,10},{10,12},{12... | collective-permute-start | bytes 258056 | tf_op jit(solution)/shard_map/ppermute | solution.py:31
  99.3 8.3 %collective-permute-start.14 = (bf16[96,448]{0,1:T(8,128)(2,1)S(1)}, bf16[96,448]{0,1:T(8,128)(2,1)S(1)}, u32[]{:S(2)}, u32[]{:S(2)}) collective-permute-start(bf16[96,448]{0,1:T(8,128)(2,1)S(1)} %get-tuple-element.24), channel_id=1, source_target_pairs={{0,4},{2,6},{4,0},{6,2},{1,5},{3,7},{5,1},{7,3},{8,12},{10,14},{12... | collective-permute-start | bytes 258056 | tf_op jit(solution)/shard_map/ppermute | solution.py:31
  102.0 5.6 %collective-permute-start.15 = (bf16[96,448]{0,1:T(8,128)(2,1)S(1)}, bf16[96,448]{0,1:T(8,128)(2,1)S(1)}, u32[]{:S(2)}, u32[]{:S(2)}) collective-permute-start(bf16[96,448]{0,1:T(8,128)(2,1)S(1)} %get-tuple-element.23), channel_id=1, source_target_pairs={{0,6},{2,0},{4,2},{6,4},{1,7},{3,1},{5,3},{7,5},{8,14},{10,8},{12,... | collective-permute-start | bytes 258056 | tf_op jit(solution)/shard_map/ppermute | solution.py:31
  108.5 17.6 %all-to-all-start.1 = ((bf16[16,6,448]{2,1,0:T(8,128)(2,1)}), bf16[16,6,448]{2,1,0:T(8,128)(2,1)S(1)}, u32[]{:S(2)}, u32[]{:S(2)}) async-start(bf16[16,6,448]{2,1,0:T(8,128)(2,1)} %reshape.543), calls=%async_computation.1 | async-start | bytes 262144 | tf_op jit(solution)/shard_map/all_to_all | solution.py:249
  118.3 84.9 %all-gather.2.cloned.1.call-start = ((), (), s32[]{:S(2)}) async-start(), calls=%async_computation.3 | async-start | bytes 14794752 | tf_op jit(solution)/shard_map/all_gather | solution.py:264
  127.5 6.8 %copy-start.6 = (bf16[6,7168]{1,0:T(8,128)(2,1)}, bf16[6,7168]{1,0:T(8,128)(2,1)S(1)}, u32[]{:S(2)}) copy-start(bf16[6,7168]{1,0:T(8,128)(2,1)S(1)} %get-tuple-element.16) | copy-start | bytes 258052
  223.9 8.4 %collective-permute-start.16 = (bf16[512,896]{1,0:T(8,128)(2,1)S(1)}, bf16[512,896]{1,0:T(8,128)(2,1)S(1)}, u32[]{:S(2)}, u32[]{:S(2)}) collective-permute-start(bf16[512,896]{1,0:T(8,128)(2,1)S(1)} %convolution_convert_fusion.3), channel_id=1, source_target_pairs={{0,1},{1,0},{2,3},{3,2},{4,5},{5,4},{6,7},{7,6},{8,9},{9,8},{10,11... | collective-permute-start | bytes 2752520 | tf_op jit(solution)/shard_map/ppermute | solution.py:35
  226.7 11.1 %collective-permute-start.18 = (bf16[512,896]{1,0:T(8,128)(2,1)}, bf16[512,896]{1,0:T(8,128)(2,1)}, u32[]{:S(2)}, u32[]{:S(2)}) collective-permute-start(bf16[512,896]{1,0:T(8,128)(2,1)} %convolution_convert_fusion.2), channel_id=1, source_target_pairs={{0,1},{1,0},{2,3},{3,2},{4,5},{5,4},{6,7},{7,6},{8,9},{9,8},{10,11... | collective-permute-start | bytes 2752520 | tf_op jit(solution)/shard_map/ppermute | solution.py:35
  229.4 11.7 %collective-permute-start.20 = (bf16[512,896]{1,0:T(8,128)(2,1)}, bf16[512,896]{1,0:T(8,128)(2,1)}, u32[]{:S(2)}, u32[]{:S(2)}) collective-permute-start(bf16[512,896]{1,0:T(8,128)(2,1)} %convolution_convert_fusion.1), channel_id=1, source_target_pairs={{0,1},{1,0},{2,3},{3,2},{4,5},{5,4},{6,7},{7,6},{8,9},{9,8},{10,11... | collective-permute-start | bytes 2752520 | tf_op jit(solution)/shard_map/ppermute | solution.py:35
  232.1 16.0 %collective-permute-start.22 = (bf16[512,896]{1,0:T(8,128)(2,1)}, bf16[512,896]{1,0:T(8,128)(2,1)S(1)}, u32[]{:S(2)}, u32[]{:S(2)}) collective-permute-start(bf16[512,896]{1,0:T(8,128)(2,1)} %convolution_convert_fusion), channel_id=1, source_target_pairs={{0,1},{1,0},{2,3},{3,2},{4,5},{5,4},{6,7},{7,6},{8,9},{9,8},{10,11... | collective-permute-start | bytes 2752520 | tf_op jit(solution)/shard_map/ppermute | solution.py:35
  234.8 25.0 %collective-permute-start.17 = (bf16[512,896]{1,0:T(8,128)(2,1)}, bf16[512,896]{1,0:T(8,128)(2,1)}, u32[]{:S(2)}, u32[]{:S(2)}) collective-permute-start(bf16[512,896]{1,0:T(8,128)(2,1)} %add_convert_fusion.3), channel_id=1, source_target_pairs={{0,4},{2,6},{4,0},{6,2},{1,5},{3,7},{5,1},{7,3},{8,12},{10,14},{12... | collective-permute-start | bytes 2752520 | tf_op jit(solution)/shard_map/ppermute | solution.py:31
  240.5 6.0 %copy-start.8 = (s32[48,8]{0,1:T(8,128)S(1)}, s32[48,8]{0,1:T(8,128)}, u32[]{:S(2)}) copy-start(s32[48,8]{0,1:T(8,128)} %param.23) | copy-start | bytes 4612
  240.5 38.3 %collective-permute-start.19 = (bf16[512,896]{1,0:T(8,128)(2,1)}, bf16[512,896]{1,0:T(8,128)(2,1)}, u32[]{:S(2)}, u32[]{:S(2)}) collective-permute-start(bf16[512,896]{1,0:T(8,128)(2,1)} %add_convert_fusion.2), channel_id=1, source_target_pairs={{0,2},{2,4},{4,6},{6,0},{1,3},{3,5},{5,7},{7,1},{8,10},{10,12},{12... | collective-permute-start | bytes 2752520 | tf_op jit(solution)/shard_map/ppermute | solution.py:31
  243.8 35.0 %collective-permute-start.21 = (bf16[512,896]{1,0:T(8,128)(2,1)}, bf16[512,896]{1,0:T(8,128)(2,1)}, u32[]{:S(2)}, u32[]{:S(2)}) collective-permute-start(bf16[512,896]{1,0:T(8,128)(2,1)} %add_convert_fusion.1), channel_id=1, source_target_pairs={{0,6},{2,0},{4,2},{6,4},{1,7},{3,1},{5,3},{7,5},{8,14},{10,8},{12,... | collective-permute-start | bytes 2752520 | tf_op jit(solution)/shard_map/ppermute | solution.py:31
  282.1 6.7 %copy-start.10 = (f32[48,8]{0,1:T(8,128)S(1)}, f32[48,8]{0,1:T(8,128)}, u32[]{:S(2)}) copy-start(f32[48,8]{0,1:T(8,128)} %param.24) | copy-start | bytes 4612
  282.1 7.3 %copy-start.7 = (bf16[6,7168]{1,0:T(8,128)(2,1)S(1)}, bf16[6,7168]{1,0:T(8,128)(2,1)}, u32[]{:S(2)}) copy-start(bf16[6,7168]{1,0:T(8,128)(2,1)} %copy-done.6) | copy-start | bytes 258052
  282.1 24.3 %all-to-all-start.2 = ((bf16[16,32,896]{2,1,0:T(8,128)(2,1)}), bf16[16,32,896]{2,1,0:T(8,128)(2,1)S(1)}, u32[]{:S(2)}, u32[]{:S(2)}) async-start(bf16[16,32,896]{2,1,0:T(8,128)(2,1)} %bitcast.26), calls=%async_computation.2 | async-start | bytes 1835008 | tf_op jit(solution)/shard_map/all_to_all | solution.py:294
  289.4 18.0 %copy-start.1 = (bf16[16,512,128]{2,1,0:T(8,128)(2,1)S(1)}, bf16[16,512,128]{2,1,0:T(8,128)(2,1)}, u32[]{:S(2)}) copy-start(bf16[16,512,128]{2,1,0:T(8,128)(2,1)} %param.19) | copy-start | bytes 6291460
Sparse Core Ops, SparseCore 0:
  128.5 74.6 all-gather.1
